TPU v7x, 32 devices: a whole 2x2x4 slice. The times are simulated.
32 devices in a mesh: region: 4 (over z), row: 8 (over y, x, core).
Axes of the slice: x: 2, y: 2, z: 4, core: 2. Of those that a mesh axis runs over, the one named last changes fastest.
Arguments:
- state0: float32 [32, 16384], P(None, ('region', 'row')), may hold values from -6 to 6
- drive: bfloat16 [32, 16384], P(None, ('region', 'row')), may hold values from -6 to 6
- cotangent: float32 [32, 16384], P(None, ('region', 'row')), may hold values from -6 to 6
- excitatory: int32 [16384], P(('region', 'row')), may hold values 0 or 1
- tile_vals: bfloat16 [128, 24, 128, 128], P(('region', 'row')), may hold values from 0.0039978027 to 0.039794922
- tile_cols: int32 [128, 24], P(('region', 'row')), may hold values from 0 to 39
- tile_count: int32 [128], P(('region', 'row')), may hold values from 1 to 24, as said below
- boundary_rows: int32 [4, 8, 4, 32], P('region', 'row'), may hold values from 0 to 511, as said below
- u_factor: bfloat16 [32, 16384], P(None, ('region', 'row')), may hold values from -1 to 1
- v_factor: bfloat16 [32, 16384], P(None, ('region', 'row')), may hold values from -0.046875 to 0.046875
Outputs:
- final_state: float32 [32, 16384], P(None, ('region', 'row'))
- grad_u: float32 [32, 16384], P(None, ('region', 'row'))
- grad_v: float32 [32, 16384], P(None, ('region', 'row'))
Inputs may be any that keep to these rules, and one draw needn't show every extreme that they name: tile_count[q] tiles of row tile q are live; its tiles j >= tile_count[q] take no part; the most, 24, is reached in every draw. `boundary_rows`: the 32 rows of one list are distinct. tile_cols[q, j] numbers a tile of 128 extended columns of the group of row tile q.
All inputs are finite; a program needn't handle non-finite values. No bound on the sum of `excitatory` on one device may be relied on, other than what follows from the above.
Results may differ from a plain program's by a relative error of at most 0.0055.
Values may be sent and summed in bfloat16 or wider, within the bound.
A program may use at most 64 MiB of HBM per device.

v0:
```python
import jax
import jax.numpy as jnp
from jax import lax
from jax.sharding import PartitionSpec as P

STEPS = 4


leak = 0.5


def apply_tiles(ext_cols, flat_cols, live_tiles, flat_tiles, row_tiles):
    batch_rows, span_cols = ext_cols.shape
    blocks = ext_cols.reshape(batch_rows, span_cols // 128, 128)[:, flat_cols, :]
    blocks = jnp.where(live_tiles[None, :, None], blocks, jnp.zeros((), blocks.dtype))
    product = jnp.einsum("bsk,sik->bsi", blocks, flat_tiles, preferred_element_type=jnp.float32)
    summed = product.reshape(batch_rows, row_tiles, -1, 128).sum(axis=2)
    return summed.reshape(batch_rows, row_tiles * 128)


def local(
    state0,
    drive,
    cotangent,
    excitatory,
    tile_vals,
    tile_cols,
    tile_count,
    boundary_rows,
    u_factor,
    v_factor,
):
    lanes = lax.axis_size("row")
    own_rows = state0.shape[1]
    own_tiles = own_rows // 128
    row_tiles = tile_vals.shape[0]
    chosen = boundary_rows.reshape(-1)
    bound_cols = chosen.shape[0]
    bound_tiles = bound_cols // 128
    per_lane = own_tiles + bound_tiles
    flat_cols = tile_cols.reshape(-1)
    live_grid = jnp.arange(tile_cols.shape[1], dtype=jnp.int32)[None, :] < tile_count[:, None]
    live_tiles = live_grid.reshape(-1)
    flat_tiles = tile_vals.reshape(-1, 128, 128)
    polarity = (2 * excitatory - 1).astype(jnp.float32)
    state = state0
    saved = []
    for moment in range(STEPS):
        rates = jnp.tanh(state)
        signed = (polarity * rates).astype(jnp.bfloat16)
        batch_rows = signed.shape[0]
        outgoing = jnp.take(signed, chosen, axis=1)
        incoming = lax.all_to_all(outgoing, "region", split_axis=1, concat_axis=1, tiled=True)
        latent = lax.psum(
            jnp.dot(signed, v_factor.T, preferred_element_type=jnp.float32), ("region", "row")
        )
        extended = jnp.concatenate([signed, incoming], axis=1)
        gathered = lax.all_gather(extended, "row", axis=1, tiled=True)
        synaptic = apply_tiles(gathered, flat_cols, live_tiles, flat_tiles, row_tiles)
        latent_b = latent.astype(jnp.bfloat16)
        lowrank = jnp.dot(latent_b, u_factor, preferred_element_type=jnp.float32)
        saved.append((rates, signed, latent_b))
        state = state + leak * (-state + synaptic + lowrank + drive.astype(jnp.float32))
    grad_u = jnp.zeros((u_factor.shape[0], own_rows), jnp.float32)
    grad_v = jnp.zeros((v_factor.shape[0], own_rows), jnp.float32)
    adjoint = cotangent
    for moment in reversed(range(STEPS)):
        rates, signed, latent_b = saved[moment]
        scaled_b = (leak * adjoint).astype(jnp.bfloat16)
        coeffs = lax.psum(
            jnp.dot(scaled_b, u_factor.T, preferred_element_type=jnp.float32), ("region", "row")
        )
        coeffs_b = coeffs.astype(jnp.bfloat16)
        batch_rows = scaled_b.shape[0]
        spread = jnp.einsum(
            "bri,rjik->brjk",
            scaled_b.reshape(batch_rows, row_tiles, 128),
            tile_vals,
            preferred_element_type=jnp.float32,
        )
        spread = jnp.where(live_grid[None, :, :, None], spread, 0.0)
        columns = jnp.zeros((batch_rows, lanes * per_lane, 128), jnp.float32)
        columns = columns.at[:, flat_cols, :].add(spread.reshape(batch_rows, -1, 128))
        summed = lax.psum_scatter(
            columns.reshape(batch_rows, -1).astype(jnp.bfloat16),
            "row",
            scatter_dimension=1,
            tiled=True,
        ).astype(jnp.float32)
        own_part = summed[:, :own_rows]
        border = summed[:, own_rows:]
        returned = lax.all_to_all(border, "region", split_axis=1, concat_axis=1, tiled=True)
        through = own_part.at[:, chosen].add(returned)
        total_signed = through + jnp.dot(coeffs_b, v_factor, preferred_element_type=jnp.float32)
        grad_u = grad_u + jnp.dot(latent_b.T, scaled_b, preferred_element_type=jnp.float32)
        grad_v = grad_v + jnp.dot(coeffs_b.T, signed, preferred_element_type=jnp.float32)
        adjoint = (1.0 - leak) * adjoint + (1.0 - rates * rates) * polarity * total_signed
    return (state, grad_u, grad_v)


def solution(mesh):
    return jax.shard_map(
        local,
        mesh=mesh,
        in_specs=(
            P(None, ("region", "row")),
            P(None, ("region", "row")),
            P(None, ("region", "row")),
            P(("region", "row")),
            P(("region", "row"), None, None, None),
            P(("region", "row"), None),
            P(("region", "row")),
            P("region", "row", None, None),
            P(None, ("region", "row")),
            P(None, ("region", "row")),
        ),
        out_specs=(
            P(None, ("region", "row")),
            P(None, ("region", "row")),
            P(None, ("region", "row")),
        ),
        check_vma=False,
    )
```

profile of v0, /device:TPU:0, one launch (start us, length us, event | category | flops | bytes accessed | tf_op | source)
XLA Modules:
  0.0 516.4 jit_solution(18197982093444526926)
XLA Ops:
  11.4 6.3 %all-to-all-start = ((bf16[4,2,512]{2,1,0:T(2,128)(2,1)}), bf16[4,2,512]{2,1,0:T(2,128)(2,1)}, u32[]{:S(2)}, u32[]{:S(2)}) async-start(bf16[4,2,512]{2,1,0:T(2,128)(2,1)} %reshape.342), calls=%async_computation | async-start | bytes 16384 | tf_op jit(solution)/shard_map/all_to_all | solution.py:53
  20.1 1.7 convolution_select_fusion.2
  22.8 13.2 %scatter_fusion = f32[32,40,128]{2,0,1:T(8,128)} fusion(f32[32,40,128]{2,0,1:T(8,128)} %broadcast.87.clone, s32[96]{0:T(128)S(1)} %fusion.52, f32[96,32,128]{2,1,0:T(8,128)} %bitcast.200), kind=kCustom, calls=%fused_computation.8 | custom fusion | flops 393216 | bytes 4718976 | tf_op jit(solution)/shard_map/scatter-add | solution.py:83
  43.5 40.8 %psum.56 = bf16[32,32]{1,0:T(8,128)(2,1)S(1)} all-reduce(f32[32,32]{1,0:T(8,128)S(1)} %fusion.60), channel_id=1, replica_groups=mesh['region'=4,'row'=8] {'region','row'}, use_global_device_ids=true, to_apply=%region_1.3 | all-reduce | flops 1024 | bytes 6144 | tf_op jit(solution)/shard_map/psum | solution.py:54
  85.2 10.4 %all_gather.12 = bf16[32,5120]{1,0:T(8,128)(2,1)S(1)} all-gather(bf16[32,640]{1,0:T(8,128)(2,1)S(1)} %pad_maximum_fusion), channel_id=1, replica_groups=mesh['region'=4,'row'=8] {'row'}, dimensions={1}, use_global_device_ids=true | all-gather | bytes 368640 | tf_op jit(solution)/shard_map/all_gather | solution.py:58
  95.7 1.7 gather_fusion
  97.4 4.1 fusion.18
  105.5 3.6 all-to-all-start.1
  109.2 39.9 %psum.57 = bf16[32,32]{1,0:T(8,128)(2,1)} all-reduce(f32[32,32]{1,0:T(8,128)S(1)} %fusion.61), channel_id=1, replica_groups=mesh['region'=4,'row'=8] {'region','row'}, use_global_device_ids=true, to_apply=%region_3.5 | all-reduce | flops 1024 | bytes 6144 | tf_op jit(solution)/shard_map/psum | solution.py:54
  149.3 10.9 %all_gather.13 = bf16[32,5120]{1,0:T(8,128)(2,1)S(1)} all-gather(bf16[32,640]{1,0:T(8,128)(2,1)S(1)} %pad_maximum_fusion.1), channel_id=1, replica_groups=mesh['region'=4,'row'=8] {'row'}, dimensions={1}, use_global_device_ids=true | all-gather | bytes 368640 | tf_op jit(solution)/shard_map/all_gather | solution.py:58
  160.3 1.7 gather_fusion.1
  162.0 4.1 fusion.16
  166.1 1.6 reduce_sum.37
  170.2 3.6 all-to-all-start.2
  173.9 40.6 %all-reduce.1 = (bf16[32,32]{1,0:T(8,128)(2,1)}, bf16[32,32]{1,0:T(8,128)(2,1)}) all-reduce(f32[32,32]{1,0:T(8,128)S(1)} %fusion.62, f32[32,32]{1,0:T(8,128)S(1)} %copy-done.26), channel_id=1, replica_groups=mesh['region'=4,'row'=8] {'region','row'}, use_global_device_ids=true, to_apply=%region_5.7 | all-reduce | flops 2048 | bytes 12288 | tf_op jit(solution)/shard_map/psum | solution.py:54
  214.7 10.5 %all_gather.14 = bf16[32,5120]{1,0:T(8,128)(2,1)S(1)} all-gather(bf16[32,640]{1,0:T(8,128)(2,1)S(1)} %pad_maximum_fusion.2), channel_id=1, replica_groups=mesh['region'=4,'row'=8] {'row'}, dimensions={1}, use_global_device_ids=true | all-gather | bytes 368640 | tf_op jit(solution)/shard_map/all_gather | solution.py:58
  225.3 1.7 gather_fusion.2
  227.0 4.1 fusion.14
  231.1 2.2 reduce_sum.38
  235.1 3.8 all-to-all-start.4
  240.8 3.9 all-to-all-done.4
  245.2 2.0 reduce
  253.0 1.7 scatter_fusion.1
  255.5 1.7 fusion.59
  259.6 38.4 %psum.61 = bf16[32,32]{1,0:T(8,128)(2,1)} all-reduce(f32[32,32]{1,0:T(8,128)S(1)} %fusion.65), channel_id=1, replica_groups=mesh['region'=4,'row'=8] {'region','row'}, use_global_device_ids=true, to_apply=%region_14.16 | all-reduce | flops 1024 | bytes 6144 | tf_op jit(solution)/shard_map/psum | solution.py:70
  298.0 2.3 convolution_select_fusion.1
  301.2 13.2 %scatter_fusion.2 = f32[32,40,128]{2,0,1:T(8,128)} fusion(f32[32,40,128]{2,0,1:T(8,128)} %broadcast.87.clone.1, s32[96]{0:T(128)S(1)} %copy-done.33, f32[96,32,128]{2,1,0:T(8,128)} %bitcast.201), kind=kCustom, calls=%fused_computation.10 | custom fusion | flops 393216 | bytes 4718976 | tf_op jit(solution)/shard_map/scatter-add | solution.py:83
  317.0 1.6 gather_fusion.7
  320.2 3.2 all-to-all-start.3
  325.0 4.0 all-to-all-done.3
  329.2 10.9 %all_gather.15 = bf16[32,5120]{1,0:T(8,128)(2,1)S(1)} all-gather(bf16[32,640]{1,0:T(8,128)(2,1)S(1)} %pad_maximum_fusion.3), channel_id=1, replica_groups=mesh['region'=4,'row'=8] {'row'}, dimensions={1}, use_global_device_ids=true | all-gather | bytes 368640 | tf_op jit(solution)/shard_map/all_gather | solution.py:58
  340.2 1.7 gather_fusion.3
  341.9 12.3 %reduce-scatter.12.cloned.1.call-done = bf16[640,32]{1,0:T(8,128)(2,1)} async-done(((bf16[5120,32]{1,0:T(8,128)(2,1)}), bf16[640,32]{1,0:T(8,128)(2,1)}) %reduce-scatter.12.cloned.1.call-update) | async-done | bytes 40976
  356.0 4.6 all-to-all-start.5
  363.0 3.3 all-to-all-done.5
  366.3 2.0 reduce.1
  374.2 1.7 scatter_fusion.3
  377.5 2.3 convolution_select_fusion
  380.8 13.2 %scatter_fusion.4 = f32[32,40,128]{2,0,1:T(8,128)} fusion(f32[32,40,128]{2,0,1:T(8,128)} %broadcast.87, s32[96]{0:T(128)S(1)} %copy-done.34, f32[96,32,128]{2,1,0:T(8,128)} %bitcast.199), kind=kCustom, calls=%fused_computation.12 | custom fusion | flops 393216 | bytes 4718976 | tf_op jit(solution)/shard_map/scatter-add | solution.py:83
  396.6 4.1 fusion.12
  400.7 2.2 reduce_sum.39
  403.0 38.6 %psum.62 = bf16[32,32]{1,0:T(8,128)(2,1)S(1)} all-reduce(f32[32,32]{1,0:T(8,128)S(1)} %fusion.66), channel_id=1, replica_groups=mesh['region'=4,'row'=8] {'region','row'}, use_global_device_ids=true, to_apply=%region_18.20 | all-reduce | flops 1024 | bytes 6144 | tf_op jit(solution)/shard_map/psum | solution.py:70
  444.3 3.8 all-to-all-start.6
  449.9 4.0 all-to-all-done.6
  459.1 1.7 scatter_fusion.5
  462.6 40.3 %all-reduce = (bf16[32,32]{1,0:T(8,128)(2,1)S(1)}, bf16[32,32]{1,0:T(8,128)(2,1)S(1)}) all-reduce(f32[32,32]{1,0:T(8,128)} %fusion.63, f32[32,32]{1,0:T(8,128)S(1)} %fusion.67), channel_id=1, replica_groups=mesh['region'=4,'row'=8] {'region','row'}, use_global_device_ids=true, to_apply=%region_7.9 | all-reduce | flops 2048 | bytes 12288 | tf_op jit(solution)/shard_map/psum | solution.py:54
  506.6 1.7 convolution_add_fusion
  508.2 1.6 fusion.2
  (215 shorter events, 73.6 us)
Async XLA Ops:
  7.2 13.0 %copy-start = (bf16[4,24,128,128]{3,2,1,0:T(8,128)(2,1)S(1)}, bf16[4,24,128,128]{3,2,1,0:T(8,128)(2,1)}, u32[]{:S(2)}) copy-start(bf16[4,24,128,128]{3,2,1,0:T(8,128)(2,1)} %param.16) | copy-start | bytes 9437188
  8.1 13.7 %copy-start.29 = (pred[128]{0:T(512)(128)(4,1)}, pred[128]{0:T(512)(128)(4,1)S(1)}, u32[]{:S(2)}) copy-start(pred[128]{0:T(512)(128)(4,1)S(1)} %compare_and_fusion) | copy-start | bytes 388
  9.7 12.2 %copy-start.6 = (bf16[32,512]{1,0:T(8,128)(2,1)}, bf16[32,512]{1,0:T(8,128)(2,1)S(1)}, u32[]{:S(2)}) copy-start(bf16[32,512]{1,0:T(8,128)(2,1)S(1)} %multiply_convert_fusion.4) | copy-start | bytes 98308
  11.4 72.9 %all-to-all-start = ((bf16[4,2,512]{2,1,0:T(2,128)(2,1)}), bf16[4,2,512]{2,1,0:T(2,128)(2,1)}, u32[]{:S(2)}, u32[]{:S(2)}) async-start(bf16[4,2,512]{2,1,0:T(2,128)(2,1)} %reshape.342), calls=%async_computation | async-start | bytes 16384 | tf_op jit(solution)/shard_map/all_to_all | solution.py:53
  17.7 215.5 %reduce-scatter.10.cloned.1.call-start = ((), (), s32[]{:S(2)}) async-start(), calls=%async_computation.10 | async-start | bytes 1474560
  18.5 23.1 %copy-start.32 = (s32[96]{0:T(128)}, s32[96]{0:T(128)S(1)}, u32[]{:S(2)}) copy-start(s32[96]{0:T(128)S(1)} %fusion.52) | copy-start | bytes 1156
  19.2 2.6 copy-start.38
  20.1 1.8 copy-start.17
  37.1 1.5 copy-start.35
  37.1 1.6 copy-start.2
  37.1 2.4 copy-start.1
  38.6 46.7 %copy-start.7 = (bf16[32,512]{1,0:T(8,128)(2,1)S(1)}, bf16[32,512]{1,0:T(8,128)(2,1)}, u32[]{:S(2)}) copy-start(bf16[32,512]{1,0:T(8,128)(2,1)} %copy-done.6) | copy-start | bytes 98308
  101.4 1.6 copy-start.15
  101.4 1.6 copy-start.21
  101.4 3.2 copy-start.30
  103.8 45.5 %copy-start.8 = (bf16[32,512]{1,0:T(8,128)(2,1)}, bf16[32,512]{1,0:T(8,128)(2,1)S(1)}, u32[]{:S(2)}) copy-start(bf16[32,512]{1,0:T(8,128)(2,1)S(1)} %get-tuple-element.11) | copy-start | bytes 98308
  105.5 43.6 %all-to-all-start.1 = ((bf16[4,2,512]{2,1,0:T(2,128)(2,1)}), bf16[4,2,512]{2,1,0:T(2,128)(2,1)S(1)}, u32[]{:S(2)}, u32[]{:S(2)}) async-start(bf16[4,2,512]{2,1,0:T(2,128)(2,1)} %reshape.344), calls=%async_computation.1 | async-start | bytes 16384 | tf_op jit(solution)/shard_map/all_to_all | solution.py:53
  166.1 1.6 copy-start.14
  166.1 1.6 copy-start.16
  166.1 1.6 copy-start.24
  166.1 3.2 copy-start.31
  166.1 7.8 %copy-start.26 = (f32[32,32]{1,0:T(8,128)S(1)}, f32[32,32]{1,0:T(8,128)}, u32[]{:S(2)}) copy-start(f32[32,32]{1,0:T(8,128)} %fusion.64) | copy-start | bytes 12292
  168.5 46.3 %copy-start.10 = (bf16[32,512]{1,0:T(8,128)(2,1)}, bf16[32,512]{1,0:T(8,128)(2,1)S(1)}, u32[]{:S(2)}) copy-start(bf16[32,512]{1,0:T(8,128)(2,1)S(1)} %get-tuple-element.13) | copy-start | bytes 98308
  170.2 44.3 %all-to-all-start.2 = ((bf16[4,2,512]{2,1,0:T(2,128)(2,1)}), bf16[4,2,512]{2,1,0:T(2,128)(2,1)S(1)}, u32[]{:S(2)}, u32[]{:S(2)}) async-start(bf16[4,2,512]{2,1,0:T(2,128)(2,1)} %reshape.346), calls=%async_computation.2 | async-start | bytes 16384 | tf_op jit(solution)/shard_map/all_to_all | solution.py:53
  231.1 7.9 %copy-start.27 = (bf16[32,32]{1,0:T(8,128)(2,1)S(1)}, bf16[32,32]{1,0:T(8,128)(2,1)}, u32[]{:S(2)}) copy-start(bf16[32,32]{1,0:T(8,128)(2,1)} %get-tuple-element.7) | copy-start | bytes 6148
  231.1 24.4 %copy-start.3 = (f32[32,512]{1,0:T(8,128)S(1)}, f32[32,512]{1,0:T(8,128)}, u32[]{:S(2)}) copy-start(f32[32,512]{1,0:T(8,128)} %get-tuple-element.14) | copy-start | bytes 196612
  235.1 9.5 %all-to-all-start.4 = ((f32[4,1,1024]{2,1,0:T(1,128)}), f32[4,1,1024]{2,1,0:T(1,128)}, u32[]{:S(2)}, u32[]{:S(2)}) async-start(f32[4,1,1024]{2,1,0:T(1,128)} %reshape.350), calls=%async_computation.4 | async-start | bytes 32768 | tf_op jit(solution)/shard_map/all_to_all | solution.py:92
  239.0 115.2 %reduce-scatter.12.cloned.1.call-start = ((), (), s32[]{:S(2)}) async-start(), calls=%async_computation.11 | async-start | bytes 1474560
  257.2 43.1 %copy-start.12 = (bf16[32,512]{1,0:T(8,128)(2,1)}, bf16[32,512]{1,0:T(8,128)(2,1)S(1)}, u32[]{:S(2)}) copy-start(bf16[32,512]{1,0:T(8,128)(2,1)S(1)} %get-tuple-element.10) | copy-start | bytes 98308
  257.2 43.1 %copy-start.18 = (bf16[32,512]{1,0:T(8,128)(2,1)}, bf16[32,512]{1,0:T(8,128)(2,1)S(1)}, u32[]{:S(2)}) copy-start(bf16[32,512]{1,0:T(8,128)(2,1)S(1)} %get-tuple-element.8) | copy-start | bytes 98308
  298.0 3.2 copy-start.33
  317.0 6.4 %copy-start.11 = (bf16[32,512]{1,0:T(8,128)(2,1)S(1)}, bf16[32,512]{1,0:T(8,128)(2,1)}, u32[]{:S(2)}) copy-start(bf16[32,512]{1,0:T(8,128)(2,1)} %copy-done.10) | copy-start | bytes 98308
  317.0 6.4 %copy-start.23 = (f32[32,512]{1,0:T(8,128)S(1)}, f32[32,512]{1,0:T(8,128)}, u32[]{:S(2)}) copy-start(f32[32,512]{1,0:T(8,128)} %fusion.68) | copy-start | bytes 196612
  317.0 6.4 %copy-start.25 = (bf16[32,32]{1,0:T(8,128)(2,1)S(1)}, bf16[32,32]{1,0:T(8,128)(2,1)}, u32[]{:S(2)}) copy-start(bf16[32,32]{1,0:T(8,128)(2,1)} %psum.61) | copy-start | bytes 6148
  317.0 7.2 %copy-start.13 = (bf16[32,512]{1,0:T(8,128)(2,1)S(1)}, bf16[32,512]{1,0:T(8,128)(2,1)}, u32[]{:S(2)}) copy-start(bf16[32,512]{1,0:T(8,128)(2,1)} %copy-done.12) | copy-start | bytes 98308
  320.2 8.8 %all-to-all-start.3 = ((bf16[4,2,512]{2,1,0:T(2,128)(2,1)}), bf16[4,2,512]{2,1,0:T(2,128)(2,1)S(1)}, u32[]{:S(2)}, u32[]{:S(2)}) async-start(bf16[4,2,512]{2,1,0:T(2,128)(2,1)} %reshape.348), calls=%async_computation.3 | async-start | bytes 16384 | tf_op jit(solution)/shard_map/all_to_all | solution.py:53
  340.2 34.0 %copy-start.36 = (s32[128]{0:T(128)S(1)}, s32[128]{0:T(128)}, u32[]{:S(2)}) copy-start(s32[128]{0:T(128)} %fusion.53) | copy-start | bytes 1540
  341.9 34.7 %copy-start.4 = (f32[32,512]{1,0:T(8,128)S(1)}, f32[32,512]{1,0:T(8,128)}, u32[]{:S(2)}) copy-start(f32[32,512]{1,0:T(8,128)} %get-tuple-element.14) | copy-start | bytes 196612
  356.0 10.3 %all-to-all-start.5 = ((f32[4,1,1024]{2,1,0:T(1,128)}), f32[4,1,1024]{2,1,0:T(1,128)}, u32[]{:S(2)}, u32[]{:S(2)}) async-start(f32[4,1,1024]{2,1,0:T(1,128)} %reshape.352), calls=%async_computation.5 | async-start | bytes 32768 | tf_op jit(solution)/shard_map/all_to_all | solution.py:92
  360.6 81.9 %reduce-scatter.14.cloned.1.call-start = ((), (), s32[]{:S(2)}) async-start(), calls=%async_computation.12 | async-start | bytes 1474560
  377.5 2.4 copy-start.19
  377.5 3.2 copy-start.34
  400.7 2.2 copy-start.20
  400.7 41.0 %copy-start.9 = (bf16[32,512]{1,0:T(8,128)(2,1)S(1)}, bf16[32,512]{1,0:T(8,128)(2,1)}, u32[]{:S(2)}) copy-start(bf16[32,512]{1,0:T(8,128)(2,1)} %copy-done.8) | copy-start | bytes 98308
  400.7 41.0 %copy-start.22 = (f32[32,512]{1,0:T(8,128)S(1)}, f32[32,512]{1,0:T(8,128)}, u32[]{:S(2)}) copy-start(f32[32,512]{1,0:T(8,128)} %convolution_add_fusion.2) | copy-start | bytes 196612
  400.7 58.4 %copy-start.37 = (s32[128]{0:T(128)S(1)}, s32[128]{0:T(128)}, u32[]{:S(2)}) copy-start(s32[128]{0:T(128)} %fusion.53) | copy-start | bytes 1540
  402.9 58.6 %copy-start.5 = (f32[32,512]{1,0:T(8,128)S(1)}, f32[32,512]{1,0:T(8,128)}, u32[]{:S(2)}) copy-start(f32[32,512]{1,0:T(8,128)} %get-tuple-element.14) | copy-start | bytes 196612
  444.3 9.5 %all-to-all-start.6 = ((f32[4,1,1024]{2,1,0:T(1,128)}), f32[4,1,1024]{2,1,0:T(1,128)}, u32[]{:S(2)}, u32[]{:S(2)}) async-start(f32[4,1,1024]{2,1,0:T(1,128)} %reshape.354), calls=%async_computation.6 | async-start | bytes 32768 | tf_op jit(solution)/shard_map/all_to_all | solution.py:92
  (1 other events, 1.4 us)
Sparse Core Ops, SparseCore 0:
  38.7 38.7 reduce-scatter.9
  317.1 36.9 reduce-scatter.11
  396.7 34.6 reduce-scatter.13
where the time goes:
time: 520 us; the launch traced here: 516 us
  blocking collectives  281 us (54%)
  other arithmetic  68.1 us (13%)
  local copies, waits for them, and re-layouts  53.4 us (10%)
  matrix products  42.6 us (8%)
  starting transfers between devices  29 us (6%)
  waiting for transfers between devices  27.5 us (5%)
  between operations  14.4 us (3%)
    psum x4, blocking collectives, local(): lax.psum(jnp.dot(signed, v_factor.T, preferred_element_type=jnp.float32),...  162 us
    psum x2, blocking collectives, local(): lax.psum(jnp.dot(scaled_b, u_factor.T, preferred_element_type=jnp.float32...  77 us
    all_gather x4, blocking collectives, local(): gathered = lax.all_gather(extended, 'row', axis=1, tiled=True)  42.7 us
    scatter-add x3, other arithmetic, local(): columns.at[:, flat_cols, :].add(spread.reshape(batch_rows, -1, 128))  39.6 us
    unnamed x98, local copies, waits for them, and re-layouts  17 us
    all_to_all x4, starting transfers between devices, local(): lax.all_to_all(outgoing, 'region', split_axis=1, concat_axis=1, tiled=True)  16.7 us
    dot_general x4, matrix products, apply_tiles(): jnp.einsum('bsk,sik->bsi', blocks, flat_tiles, preferred_element_type=jnp...  16.3 us
    all_to_all x16, local copies, waits for them, and re-layouts, local(): lax.all_to_all(border, 'region', split_axis=1, concat_axis=1, tiled=True)  12.9 us
  transfers between devices with their start and end apart: 10, of which 5 were waited for; matrix products, arithmetic and copies ran while one was open for 14% of the time, Pallas kernels for 0%

commit v1 on v0

v1 whole, which is shorter than its diff:
```python
import functools

import jax
import jax.numpy as jnp
from jax import lax
from jax.experimental import pallas as pl
from jax.experimental.pallas import tpu as pltpu
from jax.sharding import PartitionSpec as P

STEPS = 4
LEAK = 0.5
F32 = jnp.float32
BF16 = jnp.bfloat16
MESH = pl.DeviceIdType.MESH
NT = (((1,), (1,)), ((), ()))
NN = (((1,), (0,)), ((), ()))


def dense_kernel(lanes, per_lane, cols_ref, count_ref, vals_ref, own_ref, border_ref, acc):
    q = pl.program_id(0)
    own_tiles = per_lane - 1
    acc[...] = jnp.zeros_like(acc)

    def add(j, carry):
        c = cols_ref[q, j]
        acc[c] = acc[c] + vals_ref[0, j].astype(F32)
        return carry

    lax.fori_loop(0, count_ref[q], add, 0)
    for lane in range(lanes):
        for i in range(own_tiles):
            own_ref[lane, :, i * 128 : (i + 1) * 128] = acc[lane * per_lane + i].astype(BF16)
        border_ref[:, lane * 128 : (lane + 1) * 128] = acc[lane * per_lane + own_tiles].astype(BF16)


def densify(tile_vals, tile_cols, tile_count, lanes, own_rows):
    row_tiles, kmax = tile_vals.shape[:2]
    per_lane = own_rows // 128 + 1
    return pl.pallas_call(
        functools.partial(dense_kernel, lanes, per_lane),
        out_shape=(
            jax.ShapeDtypeStruct((lanes, own_rows, own_rows), BF16),
            jax.ShapeDtypeStruct((own_rows, lanes * 128), BF16),
        ),
        grid_spec=pltpu.PrefetchScalarGridSpec(
            num_scalar_prefetch=2,
            grid=(row_tiles,),
            in_specs=[pl.BlockSpec((1, kmax, 128, 128), lambda q, *_: (q, 0, 0, 0))],
            out_specs=[
                pl.BlockSpec((lanes, 128, own_rows), lambda q, *_: (0, q, 0)),
                pl.BlockSpec((128, lanes * 128), lambda q, *_: (q, 0)),
            ],
            scratch_shapes=[pltpu.VMEM((lanes * per_lane, 128, 128), F32)],
        ),
        compiler_params=pltpu.CompilerParams(vmem_limit_bytes=48 * 1024 * 1024),
    )(tile_cols, tile_count, tile_vals)


def fold(x, rank):
    shift = 64
    while shift >= rank:
        x = x + pltpu.roll(x, shift, 1)
        shift //= 2
    return x


def round_trip(x):
    return x.astype(BF16).astype(F32)


def step_kernel(
    groups,
    lanes,
    bsrc,
    state_ref,
    drive_ref,
    cot_ref,
    exc_ref,
    own_hbm,
    border_hbm,
    rows_ref,
    u_ref,
    v_ref,
    final_ref,
    gu_ref,
    gv_ref,
    a_own,
    a_border,
    pick,
    ext,
    zsend,
    zbuf,
    bbuf,
    rsend,
    rbuf,
    azsend,
    azbuf,
    rates_sv,
    signed_sv,
    scaled_sv,
    lat_sv,
    coef_sv,
    adj_sv,
    state_sv,
    load_sem,
    ext_s,
    ext_r,
    z_s,
    z_r,
    b_s,
    b_r,
    r_s,
    r_r,
    az_s,
    az_r,
):
    g = lax.axis_index("region")
    w = lax.axis_index("row")
    batch, own = state_ref.shape
    rank = u_ref.shape[0]

    load_own = pltpu.make_async_copy(own_hbm, a_own, load_sem.at[0])
    load_border = pltpu.make_async_copy(border_hbm, a_border, load_sem.at[1])
    load_own.start()
    load_border.start()

    def row_peer(d):
        return lax.rem(w + d, lanes)

    def region_peer(d):
        return lax.rem(g + d, groups)

    barrier = pltpu.get_barrier_semaphore()

    def greet_row(d, carry):
        pl.semaphore_signal(barrier, inc=1, device_id=(g, row_peer(d)), device_id_type=MESH)
        return carry

    def greet_region(d, carry):
        pl.semaphore_signal(barrier, inc=1, device_id=(region_peer(d), w), device_id_type=MESH)
        return carry

    lax.fori_loop(1, lanes, greet_row, 0)
    lax.fori_loop(1, groups, greet_region, 0)

    lane = lax.broadcasted_iota(jnp.int32, (batch, 128), 1)

    def offset(s):
        return lax.rem(lane + (128 * bsrc - bsrc * s), 128)

    def is_border(s):
        return offset(s) < bsrc

    def is_low_border(s):
        return (offset(s) >= bsrc) & (offset(s) < 2 * bsrc)

    def is_high(s):
        return (offset(s) >= 2 * bsrc) & (offset(s) < 2 * bsrc + rank)

    def is_low(s):
        return (offset(s) >= 2 * bsrc + rank) & (offset(s) < 2 * bsrc + 2 * rank)

    def is_sum(s):
        return is_high(s) | is_low(s)

    def sum_tile(x):
        high = round_trip(x)
        return jnp.where(lane < rank, x, jnp.where(lane < 2 * rank, x - high, 0.0)).astype(BF16)

    polarity = (2 * exc_ref[...] - 1).astype(F32)
    u_all = jnp.concatenate([u_ref[...]] * (128 // rank), axis=0)
    v_cols = jnp.concatenate([v_ref[...].astype(F32)] * (128 // rank), axis=0).T
    sub = lax.broadcasted_iota(jnp.int32, (own, 128), 0)
    own_lane = lax.rem(
        lax.broadcasted_iota(jnp.int32, (own, 128), 1) + (128 * bsrc - bsrc * g), 128
    )
    for s in range(groups):
        hot = jnp.where(sub == rows_ref[s : s + 1, :], 1.0, 0.0)
        pick[:, s * 128 : (s + 1) * 128] = jnp.where(own_lane < 2 * bsrc, hot, v_cols).astype(BF16)

    def row_copy(kind, t, d, src, dst):
        send, recv = kind
        return pltpu.make_async_remote_copy(
            src_ref=src,
            dst_ref=dst,
            send_sem=send.at[t, d],
            recv_sem=recv.at[t, w],
            device_id=(g, row_peer(d)),
            device_id_type=MESH,
        )

    def region_copy(kind, t, d, src, dst):
        send, recv = kind
        return pltpu.make_async_remote_copy(
            src_ref=src,
            dst_ref=dst,
            send_sem=send.at[t, d],
            recv_sem=recv.at[t, g],
            device_id=(region_peer(d), w),
            device_id_type=MESH,
        )

    def arrive(recv, t, source, ref):
        pltpu.make_async_copy(ref, ref, recv.at[t, source]).wait()

    def each(low, high, body):
        def step(d, carry):
            body(d)
            return carry

        lax.fori_loop(low, high, step, 0)

    def forward_send(t, state):
        rates = jnp.tanh(state)
        signed = (polarity * rates).astype(BF16)
        rates_sv[t] = rates
        signed_sv[t] = signed
        message = lax.dot_general(signed, pick[...], NN, preferred_element_type=F32)
        mine_low = is_low(g)
        for s in range(groups):
            tile = message[:, s * 128 : (s + 1) * 128]
            zsend[t, s] = jnp.where(mine_low, tile - round_trip(tile), tile).astype(BF16)
        each(
            1,
            groups,
            lambda d: region_copy(
                (z_s, z_r), t, d, zsend.at[t, region_peer(d)], zbuf.at[t, g]
            ).start(),
        )
        ext[t, w] = signed
        each(
            1,
            lanes,
            lambda d: row_copy((ext_s, ext_r), t, d, ext.at[t, w], ext.at[t, w]).start(),
        )
        zbuf[t, g] = zsend[t, g]

    def forward_merge(t):
        each(1, groups, lambda d: arrive(z_r, t, region_peer(d), zbuf.at[t, region_peer(d)]))
        border = jnp.zeros((batch, 128), F32)
        latent = jnp.zeros((batch, 128), F32)
        for s in range(groups):
            tile = zbuf[t, s].astype(F32)
            border = jnp.where(is_border(s), tile, border)
            latent = latent + jnp.where(is_sum(s), tile, 0.0)
        bbuf[t, w, :, 0:128] = border.astype(BF16)
        bbuf[t, w, :, 128:256] = sum_tile(fold(latent, rank))
        each(
            1,
            lanes,
            lambda d: row_copy((b_s, b_r), t, d, bbuf.at[t, w], bbuf.at[t, w]).start(),
        )

    def forward_finish(t, state):
        def gather(d, total):
            peer = row_peer(d)
            arrive(ext_r, t, peer, ext.at[t, peer])
            return total + lax.dot_general(
                ext[t, peer], a_own[peer], NT, preferred_element_type=F32
            )

        total = lax.dot_general(ext[t, w], a_own[w], NT, preferred_element_type=F32)
        total = lax.fori_loop(1, lanes, gather, total)
        each(1, lanes, lambda d: arrive(b_r, t, row_peer(d), bbuf.at[t, row_peer(d)]))
        latent = jnp.zeros((batch, 128), F32)
        tiles = []
        for lane_at in range(lanes):
            tiles.append(bbuf[t, lane_at, :, 0:128])
            latent = latent + bbuf[t, lane_at, :, 128:256].astype(F32)
        total = total + lax.dot_general(
            jnp.concatenate(tiles, axis=1), a_border[...], NT, preferred_element_type=F32
        )
        latent = round_trip(fold(latent, rank))
        lat_sv[t * batch : (t + 1) * batch, :] = latent
        total = total + lax.dot_general(
            latent[:, :rank].astype(BF16), u_ref[...], NN, preferred_element_type=F32
        )
        return state + LEAK * (-state + total + drive_ref[...].astype(F32))

    def adjoint_send(t, adjoint):
        scaled = (LEAK * adjoint).astype(BF16)
        scaled_sv[t * batch : (t + 1) * batch, :] = scaled
        coeff = sum_tile(lax.dot_general(scaled, u_all, NT, preferred_element_type=F32))
        if t == 0:
            rbuf[t, w, :, own + 128 : own + 256] = coeff
            part = pl.ds(own + 128, 128)
            each(
                1,
                lanes,
                lambda d: row_copy(
                    (r_s, r_r), t, d, rbuf.at[t, w, :, part], rbuf.at[t, w, :, part]
                ).start(),
            )
            return
        border = lax.dot_general(scaled, a_border[...], NN, preferred_element_type=F32).astype(BF16)
        for lane_at in range(lanes):
            rsend[t, lane_at, :, own : own + 128] = border[:, lane_at * 128 : (lane_at + 1) * 128]
            rsend[t, lane_at, :, own + 128 : own + 256] = coeff

        def spread(peer):
            return lax.dot_general(scaled, a_own[peer], NN, preferred_element_type=F32).astype(BF16)

        def push(d):
            peer = row_peer(d)
            rsend[t, peer, :, 0:own] = spread(peer)
            row_copy((r_s, r_r), t, d, rsend.at[t, peer], rbuf.at[t, w]).start()

        each(1, lanes, push)
        rbuf[t, w, :, 0:own] = spread(w)
        rbuf[t, w, :, own : own + 256] = rsend[t, w, :, own : own + 256]

    def adjoint_merge(t):
        low = own + 128 if t == 0 else 0
        part = pl.ds(low, own + 256 - low)
        each(
            1,
            lanes,
            lambda d: arrive(r_r, t, row_peer(d), rbuf.at[t, row_peer(d), :, part]),
        )
        summed = rbuf[t, 0, :, part].astype(F32)
        for lane_at in range(1, lanes):
            summed = summed + rbuf[t, lane_at, :, part].astype(F32)
        coeff = fold(summed[:, own + 128 - low :], rank)
        coeff_low = coeff - round_trip(coeff)
        if t == 0:
            border = border_low = jnp.zeros((batch, 128), F32)
        else:
            border = summed[:, own : own + 128]
            border_low = pltpu.roll(border - round_trip(border), bsrc, 1)
        for s in range(groups):
            tile = jnp.where(
                is_border(s),
                border,
                jnp.where(is_low_border(s), border_low, jnp.where(is_high(s), coeff, coeff_low)),
            )
            azsend[t, s] = tile.astype(BF16)
        each(
            1,
            groups,
            lambda d: region_copy(
                (az_s, az_r), t, d, azsend.at[t, region_peer(d)], azbuf.at[t, g]
            ).start(),
        )
        azbuf[t, g] = azsend[t, g]
        return None if t == 0 else summed[:, :own]

    def adjoint_finish(t, through):
        each(1, groups, lambda d: arrive(az_r, t, region_peer(d), azbuf.at[t, region_peer(d)]))
        mine = is_sum(g)
        coeff = jnp.zeros((batch, 128), F32)
        for s in range(groups):
            coeff = coeff + jnp.where(mine, azbuf[t, s].astype(F32), 0.0)
        coeff = round_trip(fold(coeff, rank))
        coef_sv[t * batch : (t + 1) * batch, :] = coeff
        if t == 0:
            return None
        home = offset(g) < 2 * bsrc
        tiles = []
        for s in range(groups):
            rest = jnp.where(is_high(g), coeff, 0.0) if s == 0 else jnp.zeros_like(coeff)
            tiles.append(jnp.where(home, azbuf[t, s].astype(F32), rest).astype(BF16))
        return through + lax.dot_general(
            jnp.concatenate(tiles, axis=1), pick[...], NT, preferred_element_type=F32
        )

    def adjoint_step(t, adjoint, total):
        rates = rates_sv[t]
        return (1.0 - LEAK) * adjoint + (1.0 - rates * rates) * polarity * total

    pl.semaphore_wait(barrier, lanes + groups - 2)

    last = STEPS - 1
    state = state_ref[...]
    forward_send(0, state)
    forward_merge(0)
    load_own.wait()
    load_border.wait()
    state = forward_finish(0, state)

    forward_send(1, state)
    adjoint_send(last, cot_ref[...])
    forward_merge(1)
    state = forward_finish(1, state)

    forward_send(2, state)
    forward_merge(2)
    adj_sv[...] = adjoint_merge(last)
    state = forward_finish(2, state)

    rates_sv[last] = jnp.tanh(state)
    state_sv[...] = state
    adjoint = adjoint_step(last, cot_ref[...], adjoint_finish(last, adj_sv[...]))
    adjoint_send(2, adjoint)
    forward_send(last, state_sv[...])
    forward_merge(last)
    through = adjoint_merge(2)
    adjoint = adjoint_step(2, adjoint, adjoint_finish(2, through))
    adjoint_send(1, adjoint)
    final_ref[...] = forward_finish(last, state_sv[...])
    through = adjoint_merge(1)
    adjoint = adjoint_step(1, adjoint, adjoint_finish(1, through))
    adjoint_send(0, adjoint)
    lat = lat_sv[...].T[:rank].astype(BF16)
    gu_ref[...] = lax.dot_general(lat, scaled_sv[...], NN, preferred_element_type=F32)
    adjoint_merge(0)
    adjoint_finish(0, None)
    coef = coef_sv[...].T[:rank].astype(BF16)
    signed_all = jnp.concatenate([signed_sv[t] for t in range(STEPS)], axis=0)
    gv_ref[...] = lax.dot_general(coef, signed_all, NN, preferred_element_type=F32)

    for t in range(STEPS):
        each(
            1,
            groups,
            lambda d: region_copy(
                (z_s, z_r), t, d, zsend.at[t, region_peer(d)], zbuf.at[t, g]
            ).wait_send(),
        )
        each(
            1,
            groups,
            lambda d: region_copy(
                (az_s, az_r), t, d, azsend.at[t, region_peer(d)], azbuf.at[t, g]
            ).wait_send(),
        )

        def drain(d):
            row_copy((ext_s, ext_r), t, d, ext.at[t, w], ext.at[t, w]).wait_send()
            row_copy((b_s, b_r), t, d, bbuf.at[t, w], bbuf.at[t, w]).wait_send()
            if t == 0:
                part = pl.ds(own + 128, 128)
                row_copy(
                    (r_s, r_r), t, d, rbuf.at[t, w, :, part], rbuf.at[t, w, :, part]
                ).wait_send()
            else:
                row_copy((r_s, r_r), t, d, rsend.at[t, row_peer(d)], rbuf.at[t, w]).wait_send()

        each(1, lanes, drain)


def local(
    state0,
    drive,
    cotangent,
    excitatory,
    tile_vals,
    tile_cols,
    tile_count,
    boundary_rows,
    u_factor,
    v_factor,
):
    lanes = lax.axis_size("row")
    groups, bsrc = boundary_rows.shape[2:]
    batch, own = state0.shape
    rank = u_factor.shape[0]
    a_own, a_border = densify(tile_vals, tile_cols, tile_count, lanes, own)
    rows = jnp.tile(boundary_rows.reshape(groups, bsrc), (1, 128 // bsrc))
    vmem = pl.BlockSpec(memory_space=pltpu.VMEM)
    hbm = pl.BlockSpec(memory_space=pl.ANY)
    dma = pltpu.SemaphoreType.DMA
    out = jax.ShapeDtypeStruct((batch, own), F32)
    grad = jax.ShapeDtypeStruct((rank, own), F32)
    return pl.pallas_call(
        functools.partial(step_kernel, groups, lanes, bsrc),
        out_shape=(out, grad, grad),
        in_specs=[vmem, vmem, vmem, vmem, hbm, hbm, vmem, vmem, vmem],
        out_specs=(vmem, vmem, vmem),
        scratch_shapes=[
            pltpu.VMEM((lanes, own, own), BF16),
            pltpu.VMEM((own, lanes * 128), BF16),
            pltpu.VMEM((own, groups * 128), BF16),
            pltpu.VMEM((STEPS, lanes, batch, own), BF16),
            pltpu.VMEM((STEPS, groups, batch, 128), BF16),
            pltpu.VMEM((STEPS, groups, batch, 128), BF16),
            pltpu.VMEM((STEPS, lanes, batch, 256), BF16),
            pltpu.VMEM((STEPS, lanes, batch, own + 256), BF16),
            pltpu.VMEM((STEPS, lanes, batch, own + 256), BF16),
            pltpu.VMEM((STEPS, groups, batch, 128), BF16),
            pltpu.VMEM((STEPS, groups, batch, 128), BF16),
            pltpu.VMEM((STEPS, batch, own), F32),
            pltpu.VMEM((STEPS, batch, own), BF16),
            pltpu.VMEM((STEPS * batch, own), BF16),
            pltpu.VMEM((STEPS * batch, 128), F32),
            pltpu.VMEM((STEPS * batch, 128), F32),
            pltpu.VMEM((batch, own), F32),
            pltpu.VMEM((batch, own), F32),
            dma((2,)),
            dma((STEPS, lanes)),
            dma((STEPS, lanes)),
            dma((STEPS, groups)),
            dma((STEPS, groups)),
            dma((STEPS, lanes)),
            dma((STEPS, lanes)),
            dma((STEPS, lanes)),
            dma((STEPS, lanes)),
            dma((STEPS, groups)),
            dma((STEPS, groups)),
        ],
        compiler_params=pltpu.CompilerParams(
            collective_id=0, has_side_effects=True, vmem_limit_bytes=60 * 1024 * 1024
        ),
    )(
        state0,
        drive,
        cotangent,
        excitatory.reshape(1, own),
        a_own,
        a_border,
        rows,
        u_factor,
        v_factor,
    )


def solution(mesh):
    return jax.shard_map(
        local,
        mesh=mesh,
        in_specs=(
            P(None, ("region", "row")),
            P(None, ("region", "row")),
            P(None, ("region", "row")),
            P(("region", "row")),
            P(("region", "row"), None, None, None),
            P(("region", "row"), None),
            P(("region", "row")),
            P("region", "row", None, None),
            P(None, ("region", "row")),
            P(None, ("region", "row")),
        ),
        out_specs=(
            P(None, ("region", "row")),
            P(None, ("region", "row")),
            P(None, ("region", "row")),
        ),
        check_vma=False,
    )
```

time: 520 us -> 81.6 us (0.16)
  blocking collectives: 281 us -> 0 us
  Pallas kernels: 0 us -> 70.6 us
  other arithmetic: 68.1 us -> 0 us
  local copies, waits for them, and re-layouts: 53.4 us -> 9.97 us
  matrix products: 42.6 us -> 0 us
  starting transfers between devices: 29 us -> 0 us
  waiting for transfers between devices: 27.5 us -> 0 us
  between operations: 14.4 us -> 0.64 us
    psum x6 -> x0, blocking collectives: 239 us -> none  [the longest x4 162 us: local(): lax.psum(jnp.dot(signed, v_factor.T, preferred_element_type=jnp.float32),...]
    pallas_call x0 -> x2, Pallas kernels: none -> 70.6 us  [the longest x1 66.6 us: local(): pl.pallas_call(functools.partial(step_kernel, groups, lanes, bsrc), out_s...]
    scatter-add x6 -> x0, other arithmetic: 44.6 us -> none  [the longest x3 39.6 us: local(): columns.at[:, flat_cols, :].add(spread.reshape(batch_rows, -1, 128))]
    all_gather x4 -> x0, blocking collectives: 42.7 us -> none  [local(): gathered = lax.all_gather(extended, 'row', axis=1, tiled=True)]
    dot_general x30 -> x0, matrix products: 42.6 us -> none  [the longest x4 16.3 us: apply_tiles(): jnp.einsum('bsk,sik->bsi', blocks, flat_tiles, preferred_element_type=jnp...]
    all_to_all x7 -> x0, starting transfers between devices: 29 us -> none  [the longest x4 16.7 us: local(): lax.all_to_all(outgoing, 'region', split_axis=1, concat_axis=1, tiled=True)]
    all_to_all x7 -> x0, waiting for transfers between devices: 15.2 us -> none  [the longest x3 11.2 us: local(): lax.all_to_all(border, 'region', split_axis=1, concat_axis=1, tiled=True)]
    all_to_all x28 -> x0, local copies, waits for them, and re-layouts: 13.7 us -> none  [the longest x16 12.9 us: local(): lax.all_to_all(border, 'region', split_axis=1, concat_axis=1, tiled=True)]
  transfers between devices with their start and end apart: 10 -> 0, of which waited for: 5 -> 0; matrix products, arithmetic and copies ran while one was open for 14% -> 0% of each run, Pallas kernels for 0% -> 0%
where the time goes in v1:
time: 81.6 us; the launch traced here: 81.2 us
  Pallas kernels  70.6 us (87%)
  local copies, waits for them, and re-layouts  9.97 us (12%)
    pallas_call x1, Pallas kernels, local(): pl.pallas_call(functools.partial(step_kernel, groups, lanes, bsrc), out_s...  66.6 us
    unnamed x11, local copies, waits for them, and re-layouts  8.62 us
    pallas_call x1, Pallas kernels, densify(): pl.pallas_call(functools.partial(dense_kernel, lanes, per_lane), out_shap...  4 us

profile of v1, /device:TPU:0, one launch (start us, length us, event | category | flops | bytes accessed | tf_op | source)
XLA Modules:
  0.0 81.2 jit_solution(4284358212907577815)
XLA Ops:
  0.6 0.7 tile.11
  1.3 0.7 tile.12.rows_ref
  2.0 0.0 copy-start
  2.0 1.9 %copy-done = bf16[4,24,128,128]{3,2,1,0:T(8,128)(2,1)S(1)} copy-done((bf16[4,24,128,128]{3,2,1,0:T(8,128)(2,1)S(1)}, bf16[4,24,128,128]{3,2,1,0:T(8,128)(2,1)}, u32[]{:S(2)}) %copy-start) | copy-done | bytes 3145752
  3.9 0.0 copy-start.2
  3.9 0.7 copy-done.2
  4.6 0.0 copy-start.3
  4.6 0.7 copy-done.3
  5.2 4.0 %shard_map.121 = (bf16[8,512,512]{2,1,0:T(8,128)(2,1)}, bf16[512,1024]{1,0:T(8,128)(2,1)S(1)}) custom-call(s32[4,24]{1,0:T(4,128)S(1)} %copy-done.2, s32[4]{0:T(128)S(1)} %copy-done.3, bf16[4,24,128,128]{3,2,1,0:T(8,128)(2,1)S(1)} %copy-done), custom_call_target="tpu_custom_call" | custom-call | tf_op jit(solution)/shard_map/pallas_call | solution.py:39
  9.2 0.0 copy-start.1
  9.2 1.0 %copy-done.1 = bf16[512,1024]{1,0:T(8,128)(2,1)} copy-done((bf16[512,1024]{1,0:T(8,128)(2,1)}, bf16[512,1024]{1,0:T(8,128)(2,1)S(1)}, u32[]{:S(2)}) %copy-start.1) | copy-done | bytes 1048600
  10.2 66.6 %shard_map.122 = (f32[32,512]{1,0:T(8,128)}, f32[32,512]{1,0:T(8,128)}, f32[32,512]{1,0:T(8,128)}) custom-call(f32[32,512]{1,0:T(8,128)} %state_ref.1, bf16[32,512]{1,0:T(8,128)(2,1)} %drive_ref.1, f32[32,512]{1,0:T(8,128)} %cot_ref.1, s32[1,512]{1,0:T(1,128)} %bitcast.2, bf16[8,512,512]{2,1,0:T(8,128)(2,1)} %get-tuple-element.5.own_hbm, ...), custom_call_target="tpu_custom_call" | custom-call | tf_op jit(solution)/shard_map/pallas_call | solution.py:464
  76.8 1.5 %copy.16 = f32[32,512]{1,0:T(8,128)} copy(f32[32,512]{1,0:T(8,128)} %get-tuple-element.10) | data formatting | bytes 131072
  78.2 1.5 %copy.17 = f32[32,512]{1,0:T(8,128)} copy(f32[32,512]{1,0:T(8,128)} %get-tuple-element.11) | data formatting | bytes 131072
  79.7 1.5 %copy.18 = f32[32,512]{1,0:T(8,128)} copy(f32[32,512]{1,0:T(8,128)} %get-tuple-element.12) | data formatting | bytes 131072
Async XLA Ops:
  2.0 1.9 %copy-start = (bf16[4,24,128,128]{3,2,1,0:T(8,128)(2,1)S(1)}, bf16[4,24,128,128]{3,2,1,0:T(8,128)(2,1)}, u32[]{:S(2)}) copy-start(bf16[4,24,128,128]{3,2,1,0:T(8,128)(2,1)} %vals_ref.1) | copy-start | bytes 9437188
  3.9 0.7 copy-start.2
  4.6 0.7 copy-start.3
  9.2 1.0 %copy-start.1 = (bf16[512,1024]{1,0:T(8,128)(2,1)}, bf16[512,1024]{1,0:T(8,128)(2,1)S(1)}, u32[]{:S(2)}) copy-start(bf16[512,1024]{1,0:T(8,128)(2,1)S(1)} %get-tuple-element.6.border_hbm) | copy-start | bytes 3145732

commit v2 on v1

--- a/solution.py
+++ b/solution.py
@@ -174,8 +174,9 @@
     own_lane = lax.rem(
         lax.broadcasted_iota(jnp.int32, (own, 128), 1) + (128 * bsrc - bsrc * g), 128
     )
+    rows = jnp.concatenate([rows_ref[...]] * (128 // bsrc), axis=1)
     for s in range(groups):
-        hot = jnp.where(sub == rows_ref[s : s + 1, :], 1.0, 0.0)
+        hot = jnp.where(sub == rows[s : s + 1, :], 1.0, 0.0)
         pick[:, s * 128 : (s + 1) * 128] = jnp.where(own_lane < 2 * bsrc, hot, v_cols).astype(BF16)
 
     def row_copy(kind, t, d, src, dst):
@@ -378,23 +379,24 @@
     state = forward_finish(0, state)
 
     forward_send(1, state)
+    forward_merge(1)
     adjoint_send(last, cot_ref[...])
-    forward_merge(1)
     state = forward_finish(1, state)
 
     forward_send(2, state)
+    through = adjoint_merge(last)
     forward_merge(2)
-    adj_sv[...] = adjoint_merge(last)
+    adj_sv[...] = adjoint_finish(last, through)
     state = forward_finish(2, state)
 
     rates_sv[last] = jnp.tanh(state)
     state_sv[...] = state
-    adjoint = adjoint_step(last, cot_ref[...], adjoint_finish(last, adj_sv[...]))
+    adjoint = adjoint_step(last, cot_ref[...], adj_sv[...])
     adjoint_send(2, adjoint)
+    through = adjoint_merge(2)
     forward_send(last, state_sv[...])
+    adjoint = adjoint_step(2, adjoint, adjoint_finish(2, through))
     forward_merge(last)
-    through = adjoint_merge(2)
-    adjoint = adjoint_step(2, adjoint, adjoint_finish(2, through))
     adjoint_send(1, adjoint)
     final_ref[...] = forward_finish(last, state_sv[...])
     through = adjoint_merge(1)
@@ -455,7 +457,7 @@
     batch, own = state0.shape
     rank = u_factor.shape[0]
     a_own, a_border = densify(tile_vals, tile_cols, tile_count, lanes, own)
-    rows = jnp.tile(boundary_rows.reshape(groups, bsrc), (1, 128 // bsrc))
+    rows = boundary_rows.reshape(groups, bsrc)
     vmem = pl.BlockSpec(memory_space=pltpu.VMEM)
     hbm = pl.BlockSpec(memory_space=pl.ANY)
     dma = pltpu.SemaphoreType.DMA

time: 81.6 us -> 79.3 us (0.972)
  local copies, waits for them, and re-layouts: 9.97 us -> 8.61 us
  Pallas kernels: 70.6 us -> 69.6 us
    pallas_call x1, Pallas kernels: 66.6 us -> 65.2 us  [local(): pl.pallas_call(functools.partial(step_kernel, groups, lanes, bsrc), out_s...]
    another operation x2 -> x0, local copies, waits for them, and re-layouts: 1.35 us -> none  [local(): rows = jnp.tile(boundary_rows.reshape(groups, bsrc), (1, 128 // bsrc))]
where the time goes in v2:
time: 79.3 us; the launch traced here: 78.8 us
  Pallas kernels  69.6 us (88%)
  local copies, waits for them, and re-layouts  8.61 us (11%)
    pallas_call x1, Pallas kernels, local(): pl.pallas_call(functools.partial(step_kernel, groups, lanes, bsrc), out_s...  65.2 us
    unnamed x11, local copies, waits for them, and re-layouts  8.61 us
    pallas_call x1, Pallas kernels, densify(): pl.pallas_call(functools.partial(dense_kernel, lanes, per_lane), out_shap...  4.39 us

profile of v2, /device:TPU:0, one launch (start us, length us, event | category | flops | bytes accessed | tf_op | source)
XLA Modules:
  0.0 78.8 jit_solution(4102757753086349425)
XLA Ops:
  0.6 0.0 copy-start
  0.6 1.9 %copy-done = bf16[4,24,128,128]{3,2,1,0:T(8,128)(2,1)S(1)} copy-done((bf16[4,24,128,128]{3,2,1,0:T(8,128)(2,1)S(1)}, bf16[4,24,128,128]{3,2,1,0:T(8,128)(2,1)}, u32[]{:S(2)}) %copy-start) | copy-done | bytes 3145752
  2.5 0.0 copy-start.2
  2.5 0.7 copy-done.2
  3.2 0.0 copy-start.3
  3.2 0.7 copy-done.3
  3.9 4.4 %shard_map.121 = (bf16[8,512,512]{2,1,0:T(8,128)(2,1)}, bf16[512,1024]{1,0:T(8,128)(2,1)S(1)}) custom-call(s32[4,24]{1,0:T(4,128)S(1)} %copy-done.2, s32[4]{0:T(128)S(1)} %copy-done.3, bf16[4,24,128,128]{3,2,1,0:T(8,128)(2,1)S(1)} %copy-done), custom_call_target="tpu_custom_call" | custom-call | tf_op jit(solution)/shard_map/pallas_call | solution.py:39
  8.2 0.0 copy-start.1
  8.2 1.0 %copy-done.1 = bf16[512,1024]{1,0:T(8,128)(2,1)} copy-done((bf16[512,1024]{1,0:T(8,128)(2,1)}, bf16[512,1024]{1,0:T(8,128)(2,1)S(1)}, u32[]{:S(2)}) %copy-start.1) | copy-done | bytes 1048600
  9.2 65.2 %shard_map.122 = (f32[32,512]{1,0:T(8,128)}, f32[32,512]{1,0:T(8,128)}, f32[32,512]{1,0:T(8,128)}) custom-call(f32[32,512]{1,0:T(8,128)} %state_ref.1, bf16[32,512]{1,0:T(8,128)(2,1)} %drive_ref.1, f32[32,512]{1,0:T(8,128)} %cot_ref.1, s32[1,512]{1,0:T(1,128)} %bitcast.2, bf16[8,512,512]{2,1,0:T(8,128)(2,1)} %get-tuple-element.5.own_hbm, ...), custom_call_target="tpu_custom_call" | custom-call | tf_op jit(solution)/shard_map/pallas_call | solution.py:466
  74.4 1.5 %copy.16 = f32[32,512]{1,0:T(8,128)} copy(f32[32,512]{1,0:T(8,128)} %get-tuple-element.10) | data formatting | bytes 131072
  75.9 1.5 %copy.17 = f32[32,512]{1,0:T(8,128)} copy(f32[32,512]{1,0:T(8,128)} %get-tuple-element.11) | data formatting | bytes 131072
  77.4 1.5 %copy.18 = f32[32,512]{1,0:T(8,128)} copy(f32[32,512]{1,0:T(8,128)} %get-tuple-element.12) | data formatting | bytes 131072
Async XLA Ops:
  0.6 1.9 %copy-start = (bf16[4,24,128,128]{3,2,1,0:T(8,128)(2,1)S(1)}, bf16[4,24,128,128]{3,2,1,0:T(8,128)(2,1)}, u32[]{:S(2)}) copy-start(bf16[4,24,128,128]{3,2,1,0:T(8,128)(2,1)} %vals_ref.1) | copy-start | bytes 9437188
  2.5 0.7 copy-start.2
  3.2 0.7 copy-start.3
  8.2 1.0 %copy-start.1 = (bf16[512,1024]{1,0:T(8,128)(2,1)}, bf16[512,1024]{1,0:T(8,128)(2,1)S(1)}, u32[]{:S(2)}) copy-start(bf16[512,1024]{1,0:T(8,128)(2,1)S(1)} %get-tuple-element.6.border_hbm) | copy-start | bytes 3145732

commit v3 on v2

--- a/solution.py
+++ b/solution.py
@@ -179,6 +179,9 @@
         hot = jnp.where(sub == rows[s : s + 1, :], 1.0, 0.0)
         pick[:, s * 128 : (s + 1) * 128] = jnp.where(own_lane < 2 * bsrc, hot, v_cols).astype(BF16)
 
+    half = lanes // 2
+    peer_groups = (range(1, half), range(half, lanes))
+
     def row_copy(kind, t, d, src, dst):
         send, recv = kind
         return pltpu.make_async_remote_copy(
@@ -261,7 +264,16 @@
             )
 
         total = lax.dot_general(ext[t, w], a_own[w], NT, preferred_element_type=F32)
-        total = lax.fori_loop(1, lanes, gather, total)
+        if lanes <= 8:
+            for batch_of in peer_groups:
+                for d in batch_of:
+                    arrive(ext_r, t, row_peer(d), ext.at[t, row_peer(d)])
+                for d in batch_of:
+                    total = total + lax.dot_general(
+                        ext[t, row_peer(d)], a_own[row_peer(d)], NT, preferred_element_type=F32
+                    )
+        else:
+            total = lax.fori_loop(1, lanes, gather, total)
         each(1, lanes, lambda d: arrive(b_r, t, row_peer(d), bbuf.at[t, row_peer(d)]))
         latent = jnp.zeros((batch, 128), F32)
         tiles = []
@@ -306,7 +318,15 @@
             rsend[t, peer, :, 0:own] = spread(peer)
             row_copy((r_s, r_r), t, d, rsend.at[t, peer], rbuf.at[t, w]).start()
 
-        each(1, lanes, push)
+        if lanes <= 8:
+            for batch_of in peer_groups:
+                for d in batch_of:
+                    rsend[t, row_peer(d), :, 0:own] = spread(row_peer(d))
+                for d in batch_of:
+                    peer = row_peer(d)
+                    row_copy((r_s, r_r), t, d, rsend.at[t, peer], rbuf.at[t, w]).start()
+        else:
+            each(1, lanes, push)
         rbuf[t, w, :, 0:own] = spread(w)
         rbuf[t, w, :, own : own + 256] = rsend[t, w, :, own : own + 256]
 

time: 79.3 us -> 77.2 us (0.974)
  Pallas kernels: 69.6 us -> 67.4 us
    pallas_call x1, Pallas kernels: 65.2 us -> 63.3 us  [local(): pl.pallas_call(functools.partial(step_kernel, groups, lanes, bsrc), out_s...]
where the time goes in v3:
time: 77.2 us; the launch traced here: 76.7 us
  Pallas kernels  67.4 us (87%)
  local copies, waits for them, and re-layouts  8.61 us (11%)
    pallas_call x1, Pallas kernels, local(): pl.pallas_call(functools.partial(step_kernel, groups, lanes, bsrc), out_s...  63.3 us
    unnamed x11, local copies, waits for them, and re-layouts  8.61 us
    pallas_call x1, Pallas kernels, densify(): pl.pallas_call(functools.partial(dense_kernel, lanes, per_lane), out_shap...  4.1 us

profile of v3, /device:TPU:0, one launch (start us, length us, event | category | flops | bytes accessed | tf_op | source)
XLA Modules:
  0.0 76.7 jit_solution(2806739400326343893)
XLA Ops:
  0.6 0.0 copy-start
  0.6 1.9 %copy-done = bf16[4,24,128,128]{3,2,1,0:T(8,128)(2,1)S(1)} copy-done((bf16[4,24,128,128]{3,2,1,0:T(8,128)(2,1)S(1)}, bf16[4,24,128,128]{3,2,1,0:T(8,128)(2,1)}, u32[]{:S(2)}) %copy-start) | copy-done | bytes 3145752
  2.5 0.0 copy-start.2
  2.5 0.7 copy-done.2
  3.2 0.0 copy-start.3
  3.2 0.7 copy-done.3
  3.9 4.1 %shard_map.121 = (bf16[8,512,512]{2,1,0:T(8,128)(2,1)}, bf16[512,1024]{1,0:T(8,128)(2,1)S(1)}) custom-call(s32[4,24]{1,0:T(4,128)S(1)} %copy-done.2, s32[4]{0:T(128)S(1)} %copy-done.3, bf16[4,24,128,128]{3,2,1,0:T(8,128)(2,1)S(1)} %copy-done), custom_call_target="tpu_custom_call" | custom-call | tf_op jit(solution)/shard_map/pallas_call | solution.py:39
  8.0 0.0 copy-start.1
  8.0 1.0 %copy-done.1 = bf16[512,1024]{1,0:T(8,128)(2,1)} copy-done((bf16[512,1024]{1,0:T(8,128)(2,1)}, bf16[512,1024]{1,0:T(8,128)(2,1)S(1)}, u32[]{:S(2)}) %copy-start.1) | copy-done | bytes 1048600
  8.9 63.3 %shard_map.122 = (f32[32,512]{1,0:T(8,128)}, f32[32,512]{1,0:T(8,128)}, f32[32,512]{1,0:T(8,128)}) custom-call(f32[32,512]{1,0:T(8,128)} %state_ref.1, bf16[32,512]{1,0:T(8,128)(2,1)} %drive_ref.1, f32[32,512]{1,0:T(8,128)} %cot_ref.1, s32[1,512]{1,0:T(1,128)} %bitcast.2, bf16[8,512,512]{2,1,0:T(8,128)(2,1)} %get-tuple-element.5.own_hbm, ...), custom_call_target="tpu_custom_call" | custom-call | tf_op jit(solution)/shard_map/pallas_call | solution.py:486
  72.3 1.5 %copy.16 = f32[32,512]{1,0:T(8,128)} copy(f32[32,512]{1,0:T(8,128)} %get-tuple-element.10) | data formatting | bytes 131072
  73.8 1.5 %copy.17 = f32[32,512]{1,0:T(8,128)} copy(f32[32,512]{1,0:T(8,128)} %get-tuple-element.11) | data formatting | bytes 131072
  75.2 1.5 %copy.18 = f32[32,512]{1,0:T(8,128)} copy(f32[32,512]{1,0:T(8,128)} %get-tuple-element.12) | data formatting | bytes 131072
Async XLA Ops:
  0.6 1.9 %copy-start = (bf16[4,24,128,128]{3,2,1,0:T(8,128)(2,1)S(1)}, bf16[4,24,128,128]{3,2,1,0:T(8,128)(2,1)}, u32[]{:S(2)}) copy-start(bf16[4,24,128,128]{3,2,1,0:T(8,128)(2,1)} %vals_ref.1) | copy-start | bytes 9437188
  2.5 0.7 copy-start.2
  3.2 0.7 copy-start.3
  8.0 1.0 %copy-start.1 = (bf16[512,1024]{1,0:T(8,128)(2,1)}, bf16[512,1024]{1,0:T(8,128)(2,1)S(1)}, u32[]{:S(2)}) copy-start(bf16[512,1024]{1,0:T(8,128)(2,1)S(1)} %get-tuple-element.6.border_hbm) | copy-start | bytes 3145732
